TPU v7x, 32 devices: a whole 2x2x4 slice. The times are simulated.
32 devices in a mesh: view: 2 (over x), gz: 16 (over z, y, core).
Axes of the slice: x: 2, y: 2, z: 4, core: 2. Of those that a mesh axis runs over, the one named last changes fastest.
Arguments:
- estimate: float32 [512, 128, 128], P('gz'), may hold values from 0.25 to 4
- raw_bricks: bfloat16 [2, 8192, 4, 2, 128], P('view', 'gz'), may hold values from 0.25 to 4
- brick_slab: int32 [2, 8192, 1], P('view', 'gz'), may hold values from 0 to 15; in each aligned block of 512 rows (0 to 511, 512 to 1023, ..., all dimensions but the last counted through in order) at most 64 rows name the same one
- brick_pos: int32 [2, 8192], P('view', 'gz'), may hold values from 0 to 511
- off_z: int32 [2, 4], P('view'), may hold values from -1 to 3
- frac_z: float32 [2, 4], P('view'), may hold values from 0 to 1
- off_y: int32 [2, 2], P('view'), may hold values from -1 to 1
- frac_y: float32 [2, 2], P('view'), may hold values from 0 to 1
- off_x: int32 [2, 128], P('view'), may hold values from -1 to 127
- frac_x: float32 [2, 128], P('view'), may hold values from 0 to 1
- psf_z: float32 [2, 64], P('view'), may hold values from 0.05 to 1
- psf_y: float32 [2, 16], P('view'), may hold values from 0.05 to 1
- psf_x: float32 [2, 16], P('view'), may hold values from 0.05 to 1
Outputs:
- new_estimate: float32 [512, 128, 128], P('gz', 'view')
Inputs may be any that keep to these rules, and one draw needn't show every extreme that they name: `brick_slab`: in every view, the 512 bricks held by one device (an aligned block) name any one slab at most 64 times, a bound that some block reaches.
All inputs are finite; a program needn't handle non-finite values.
Results may differ from a plain program's by a relative error of at most 0.00043.
Values may be sent and summed in bfloat16 or wider, within the bound.
A program may use at most 64 MiB of HBM per device.

v0:
```python
import jax
import jax.numpy as jnp
from jax import lax
from jax.sharding import PartitionSpec as P


def with_halo(cells, sides, width):
    for axis, dim in sides:
        count = lax.axis_size(axis)
        ends = count - 1
        head = lax.slice_in_dim(cells, 0, width, axis=dim)
        tail = lax.slice_in_dim(cells, cells.shape[dim] - width, cells.shape[dim], axis=dim)
        cells = jnp.concatenate(
            [
                lax.ppermute(tail, axis, [(i, (i + 1) % count) for i in range(ends)]),
                cells,
                lax.ppermute(head, axis, [((i + 1) % count, i) for i in range(ends)]),
            ],
            axis=dim,
        )
    return cells


def rounded_weights(values):
    return lax.optimization_barrier(values.astype(jnp.bfloat16)).astype(jnp.float32)


def weight_table(offsets, fractions, length):
    source_rows = jnp.arange(length, dtype=jnp.int32)[:, None]
    low_weight = rounded_weights(1.0 - fractions)[None, :]
    high_weight = rounded_weights(fractions)[None, :]
    table = jnp.where(source_rows == offsets[None, :], low_weight, jnp.float32(0.0))
    return table + jnp.where(source_rows == offsets[None, :] + 1, high_weight, jnp.float32(0.0))


def band_table(kernel, row_count, col_count, start_tap, direction):
    normed = kernel / jnp.sum(kernel)
    distance = (
        jnp.arange(col_count, dtype=jnp.int32)[None, :]
        - jnp.arange(row_count, dtype=jnp.int32)[:, None]
    )
    which_tap = direction * distance + start_tap
    table = jnp.zeros((row_count, col_count), jnp.float32)
    for tap_index in range(kernel.shape[0]):
        table = table + jnp.where(which_tap == tap_index, normed[tap_index], jnp.float32(0.0))
    return table.astype(jnp.bfloat16)


def resample_bricks(bricks, table_x, table_zy):
    shape_in = bricks.shape
    col_count = shape_in[-1]
    along_x = jnp.dot(
        bricks.reshape(-1, col_count), table_x, preferred_element_type=jnp.float32
    ).astype(jnp.bfloat16)
    along_x = along_x.reshape(-1, table_zy.shape[0], col_count)
    mixed = jnp.einsum("qp,nqx->npx", table_zy, along_x, preferred_element_type=jnp.float32)
    return mixed.astype(jnp.bfloat16).reshape(shape_in)


def separable(padded_block, table_z, table_y, table_x, out_shape):
    along_z = jnp.dot(
        table_z, padded_block.reshape(padded_block.shape[0], -1), preferred_element_type=jnp.float32
    )
    along_z = along_z.astype(jnp.bfloat16).reshape(out_shape)
    along_y = jnp.einsum(
        "ij,zjx->zix", table_y, along_z, preferred_element_type=jnp.float32
    ).astype(jnp.bfloat16)
    result = jnp.dot(along_y.reshape(-1, out_shape[2]), table_x, preferred_element_type=jnp.float32)
    return result.reshape(out_shape)


def shards(
    estimate,
    raw_bricks,
    brick_slab,
    brick_pos,
    off_z,
    frac_z,
    off_y,
    frac_y,
    off_x,
    frac_x,
    psf_z,
    psf_y,
    psf_x,
):
    plane_count, row_count, col_count = estimate.shape
    brick_count = raw_bricks.shape[1]
    brick_depth = raw_bricks.shape[2]
    brick_height = raw_bricks.shape[3]
    brick_cells = brick_depth * brick_height
    slab_count = lax.axis_size("gz")
    capacity = max(2, 2 * brick_count // slab_count)
    slot_total = slab_count * capacity
    block_planes = plane_count // brick_depth
    block_rows = row_count // brick_height
    place_total = block_planes * block_rows
    halo_width = psf_z.shape[1] // 2
    lateral = psf_x.shape[1] // 2
    table_x = weight_table(off_x[0], frac_x[0], col_count).astype(jnp.bfloat16)
    table_z = weight_table(off_z[0], frac_z[0], brick_depth)
    table_y = weight_table(off_y[0], frac_y[0], brick_height)
    table_zy = (
        jnp.einsum("ac,bd->abcd", table_z, table_y)
        .reshape(brick_cells, brick_cells)
        .astype(jnp.bfloat16)
    )
    destination = brick_slab[0, :, 0]
    positions = brick_pos[0]
    member = (destination[:, None] == jnp.arange(slab_count, dtype=jnp.int32)[None, :]).astype(
        jnp.int32
    )
    earlier = jnp.cumsum(member, axis=0) - member
    order_within = jnp.sum(earlier * member, axis=1)
    slot_of = destination * capacity + order_within
    chosen = slot_of[None, :] == jnp.arange(slot_total, dtype=jnp.int32)[:, None]
    slot_positions = jnp.max(jnp.where(chosen, positions[None, :], -1), axis=1).reshape(
        slab_count, capacity
    )
    selector = chosen.astype(jnp.bfloat16)
    own_bricks = raw_bricks[0].reshape(brick_count, brick_cells, col_count)
    outgoing = jnp.dot(
        selector, own_bricks.reshape(brick_count, -1), preferred_element_type=jnp.float32
    )
    outgoing = outgoing.astype(jnp.bfloat16).reshape(slab_count, capacity, brick_cells, col_count)
    arrived = resample_bricks(
        lax.all_to_all(outgoing, "gz", split_axis=0, concat_axis=0, tiled=True), table_x, table_zy
    )
    arrived_positions = lax.all_to_all(
        slot_positions, "gz", split_axis=0, concat_axis=0, tiled=True
    )
    placer = (
        arrived_positions.reshape(-1)[None, :] == jnp.arange(place_total, dtype=jnp.int32)[:, None]
    ).astype(jnp.bfloat16)
    placed = jnp.dot(placer, arrived.reshape(slot_total, -1), preferred_element_type=jnp.float32)
    placed = placed.reshape(block_planes, block_rows, brick_depth, brick_height, col_count)
    joined = 1.0 + placed.transpose(0, 2, 1, 3, 4).reshape(plane_count, row_count, col_count)
    out_shape = (plane_count, row_count, col_count)
    forward_z = band_table(psf_z[0], plane_count, plane_count + 2 * halo_width, 0, 1)
    backward_z = band_table(psf_z[0], plane_count, plane_count + 2 * halo_width, 2 * halo_width, -1)
    forward_y = band_table(psf_y[0], row_count, row_count, lateral, 1)
    backward_y = band_table(psf_y[0], row_count, row_count, lateral, -1)
    forward_x = band_table(psf_x[0], col_count, col_count, lateral, -1)
    backward_x = band_table(psf_x[0], col_count, col_count, lateral, 1)
    estimate_b = estimate.astype(jnp.bfloat16)
    padded = with_halo(estimate_b, (("gz", 0),), halo_width)
    blurred = separable(padded, forward_z, forward_y, forward_x, out_shape)
    ratio = (joined / blurred).astype(jnp.bfloat16)
    ratio_padded = with_halo(ratio, (("gz", 0),), halo_width)
    correction = separable(ratio_padded, backward_z, backward_y, backward_x, out_shape)
    view_count = lax.axis_size("view")
    share_rows = row_count // view_count
    first_row = lax.axis_index("view") * share_rows
    part_total = lax.psum_scatter(correction, "view", scatter_dimension=1, tiled=True)
    part_estimate = lax.dynamic_slice_in_dim(estimate, first_row, share_rows, 1)
    return part_estimate * part_total / view_count


def solution(mesh):
    in_specs = (
        P("gz", None, None),
        P("view", "gz", None, None, None),
        P("view", "gz", None),
        P("view", "gz"),
        P("view", None),
        P("view", None),
        P("view", None),
        P("view", None),
        P("view", None),
        P("view", None),
        P("view", None),
        P("view", None),
        P("view", None),
    )
    out_specs = P("gz", "view", None)
    return jax.shard_map(shards, mesh=mesh, in_specs=in_specs, out_specs=out_specs, check_vma=False)
```

profile of v0, /device:TPU:12, one launch (start us, length us, event | category | flops | bytes accessed | tf_op | source)
XLA Modules:
  0.0 265.5 jit_solution(11031567387888439407)
XLA Ops:
  6.5 1.8 convert_element_type.159
  8.4 1.9 collective-permute-start
  10.3 3.6 %collective-permute-start.1 = (bf16[32,128,128]{2,1,0:T(8,128)(2,1)S(1)}, bf16[32,128,128]{2,1,0:T(8,128)(2,1)}, u32[]{:S(2)}, u32[]{:S(2)}) collective-permute-start(bf16[32,128,128]{2,1,0:T(8,128)(2,1)S(1)} %convert_element_type.159), channel_id=1, source_target_pairs={{1,0},{2,1},{3,2},{4,3},{5,4},{6,5},{7,6},{8,7},{9,8},{10,9},{11,1... | collective-permute-start | bytes 3145736 | tf_op jit(solution)/shard_map/ppermute | solution.py:17
  14.0 1.2 reduce-window.6
  15.9 0.7 all_to_all.9
  16.6 6.2 %all-to-all-start = ((s32[16,1,64]{2,1,0:T(1,128)}), s32[16,1,64]{2,1,0:T(1,128)S(1)}, u32[]{:S(2)}, u32[]{:S(2)}) async-start(s32[16,1,64]{2,1,0:T(1,128)} %all_to_all.9), calls=%async_computation | async-start | bytes 16384 | tf_op jit(solution)/shard_map/all_to_all | solution.py:129
  22.8 0.8 reshape_reshape_squeeze.3
  23.6 1.3 convert_bitcast_fusion
  24.8 2.0 copy.36
  26.8 9.1 %all-to-all-done = s32[16,1,64]{2,1,0:T(1,128)S(1)} async-done(((s32[16,1,64]{2,1,0:T(1,128)}), s32[16,1,64]{2,1,0:T(1,128)S(1)}, u32[]{:S(2)}, u32[]{:S(2)}) %all-to-all-start) | async-done | bytes 4128 | tf_op jit(solution)/shard_map/all_to_all | solution.py:129
  36.0 6.2 %all-to-all-start.1 = ((bf16[16,64,8,128]{3,2,1,0:T(8,128)(2,1)}), bf16[16,64,8,128]{3,2,1,0:T(8,128)(2,1)S(1)}, u32[]{:S(2)}, u32[]{:S(2)}) async-start(bf16[16,64,8,128]{3,2,1,0:T(8,128)(2,1)} %bitcast.224), calls=%async_computation.1 | async-start | bytes 4194304 | tf_op jit(solution)/shard_map/all_to_all | solution.py:127
  46.5 0.7 fusion.847
  47.8 0.7 fusion.848
  48.5 0.7 fusion.849
  49.3 0.7 fusion.850
  50.0 0.7 fusion.851
  52.0 1.7 pad_maximum_fusion
  53.7 42.2 %fusion.18 = bf16[4,8,128,128]{3,1,2,0:T(8,128)(2,1)S(1)} fusion(bf16[12,8,128,128]{3,2,1,0:T(8,128)(2,1)S(1)} %bitcast.221, f32[]{:T(128)} %bitcast.63, f32[]{:T(128)} %bitcast.62, f32[]{:T(128)} %bitcast.61, f32[]{:T(128)} %bitcast.60, f32[]{:T(128)} %bitcast.59, f32[]{:T(128)} %bitcast.58, f32[]{:T(128)} %bitcast.57, f32[]{:T(128)} %bitcast.56, ...), kind=kOutput, calls=%fused_computation.27 | convolution fusion | flops 101780480 | bytes 4194560 | tf_op jit(solution)/shard_map/dot_general | solution.py:61
  96.1 2.7 %fusion.10 = bf16[1024,128,8]{1,2,0:T(8,128)(2,1)} fusion(bf16[8192,128]{1,0:T(8,128)(2,1)S(1)} %bitcast.222, f32[128]{0:T(128)S(1)} %convert_element_type.138, s32[128]{0:T(128)S(1)} %add_bitcast_fusion.4, f32[128]{0:T(128)S(1)} %convert_element_type.135, s32[128]{0:T(128)S(1)} %bitcast.234, bf16[8,8]{1,0:T(8,128)(2,1)S(1)} %convert_element_type.155), kind=kOutput, calls=%fused_computation.21 | convolution fusion | flops 287408128 | bytes 4196480 | tf_op jit(solution)/shard_map/qp,nqx->npx/dot_general | solution.py:56
  98.8 2.2 copy.56
  101.0 2.6 copy.22
  103.6 2.9 %add_bitcast_fusion = f32[8,4,64,2,128]{4,2,3,1,0:T(8,128)S(1)} fusion(bf16[4,2,128,1024,1]{3,2,1,0,4:T(8,128)(2,1)} %bitcast.228, s32[8,64]{1,0:T(8,128)S(1)} %multiply_add_fusion.2, s32[1024]{0:T(1024)S(1)} %eq.930), kind=kOutput, calls=%fused_computation.13 | convolution fusion | flops 1074790400 | bytes 4200448 | tf_op jit(solution)/shard_map/dot_general | solution.py:135
  106.5 1.7 copy.23
  108.2 21.9 %divide_convert_fusion = bf16[32,128,128]{2,1,0:T(8,128)(2,1)} fusion(f32[32,128,128]{2,1,0:T(8,128)S(1)} %bitcast.227, bf16[32,128,128]{2,1,0:T(8,128)(2,1)S(1)} %bitcast.229, f32[]{:T(128)} %bitcast.125, f32[]{:T(128)} %bitcast.124, f32[]{:T(128)} %bitcast.123, f32[]{:T(128)} %bitcast.122, f32[]{:T(128)} %bitcast.121, f32[]{:T(128)} %bitcast.120, ...), kind=kOutput, calls=%fused_computation.12 | convolution fusion | flops 271663104 | bytes 4194432 | tf_op jit(solution)/shard_map/dot_general | solution.py:68
  130.1 2.0 collective-permute-start.2
  132.1 3.7 %collective-permute-start.3 = (bf16[32,128,128]{2,1,0:T(8,128)(2,1)}, bf16[32,128,128]{2,1,0:T(8,128)(2,1)S(1)}, u32[]{:S(2)}, u32[]{:S(2)}) collective-permute-start(bf16[32,128,128]{2,1,0:T(8,128)(2,1)} %divide_convert_fusion), channel_id=1, source_target_pairs={{1,0},{2,1},{3,2},{4,3},{5,4},{6,5},{7,6},{8,7},{9,8},{10,9},{11,1... | collective-permute-start | bytes 3145736 | tf_op jit(solution)/shard_map/ppermute | solution.py:17
  135.9 21.8 %collective-permute-done.2 = bf16[32,128,128]{2,1,0:T(8,128)(2,1)S(1)} collective-permute-done((bf16[32,128,128]{2,1,0:T(8,128)(2,1)}, bf16[32,128,128]{2,1,0:T(8,128)(2,1)S(1)}, u32[]{:S(2)}, u32[]{:S(2)}) %collective-permute-start.2) | collective-permute-done | bytes 1048608 | tf_op jit(solution)/shard_map/ppermute | solution.py:15
  157.6 1.4 pad_maximum_fusion.1
  159.1 42.2 %fusion.21 = bf16[4,8,128,128]{3,1,2,0:T(8,128)(2,1)S(1)} fusion(bf16[12,8,128,128]{3,2,1,0:T(8,128)(2,1)S(1)} %bitcast.220, f32[]{:T(128)} %bitcast.63, f32[]{:T(128)} %bitcast.62, f32[]{:T(128)} %bitcast.61, f32[]{:T(128)} %bitcast.60, f32[]{:T(128)} %bitcast.59, f32[]{:T(128)} %bitcast.58, f32[]{:T(128)} %bitcast.57, f32[]{:T(128)} %bitcast.56, ...), kind=kOutput, calls=%fused_computation.28 | convolution fusion | flops 101786624 | bytes 4194560 | tf_op jit(solution)/shard_map/dot_general | solution.py:61
  201.5 22.4 %fusion.17 = f32[32,128,128]{2,1,0:T(8,128)} fusion(bf16[32,128,128]{2,1,0:T(8,128)(2,1)S(1)} %bitcast.226, f32[]{:T(128)} %bitcast.125, f32[]{:T(128)} %bitcast.124, f32[]{:T(128)} %bitcast.123, f32[]{:T(128)} %bitcast.122, f32[]{:T(128)} %bitcast.121, f32[]{:T(128)} %bitcast.120, f32[]{:T(128)} %bitcast.119, f32[]{:T(128)} %bitcast.118, f32[]{:T(128)} %bitcast.117, ...), kind=kOutput, calls=%fused_computation.26 | convolution fusion | flops 270614528 | bytes 3145856 | tf_op jit(solution)/shard_map/dot_general | solution.py:68
  223.9 32.3 %reduce-scatter.2.cloned.1.call-done = f32[32,64,128]{2,1,0:T(8,128)} async-done(((f32[32,128,128]{2,1,0:T(8,128)}), f32[32,64,128]{2,1,0:T(8,128)}) %reduce-scatter.2.cloned.1.call-update) | async-done | bytes 1048592 | tf_op jit(solution)/shard_map/reduce_scatter | solution.py:154
  256.3 2.4 multiply_multiply_fusion
  (68 shorter events, 7.3 us)
Async XLA Ops:
  6.5 7.4 %copy-start.2 = (s32[1,512,1]{1,2,0:T(1,128)S(1)}, s32[1,512,1]{1,2,0:T(1,128)}, u32[]{:S(2)}) copy-start(s32[1,512,1]{1,2,0:T(1,128)} %param.15) | copy-start | bytes 6148
  6.5 9.0 %copy-start.3 = (s32[1,512]{1,0:T(1,128)S(1)}, s32[1,512]{1,0:T(1,128)}, u32[]{:S(2)}) copy-start(s32[1,512]{1,0:T(1,128)} %param.16) | copy-start | bytes 6148
  6.5 16.3 %copy-start.1 = (bf16[1,512,4,2,128]{4,3,2,1,0:T(2,128)(2,1)S(1)}, bf16[1,512,4,2,128]{4,3,2,1,0:T(2,128)(2,1)}, u32[]{:S(2)}) copy-start(bf16[1,512,4,2,128]{4,3,2,1,0:T(2,128)(2,1)} %param.14) | copy-start | bytes 3145732
  8.4 43.6 %collective-permute-start = (bf16[32,128,128]{2,1,0:T(8,128)(2,1)S(1)}, bf16[32,128,128]{2,1,0:T(8,128)(2,1)}, u32[]{:S(2)}, u32[]{:S(2)}) collective-permute-start(bf16[32,128,128]{2,1,0:T(8,128)(2,1)S(1)} %convert_element_type.159), channel_id=1, source_target_pairs={{0,1},{1,2},{2,3},{3,4},{4,5},{5,6},{6,7},{7,8},{8,9},{9,10},{10,1... | collective-permute-start | bytes 3145736 | tf_op jit(solution)/shard_map/ppermute | solution.py:15
  10.3 41.7 %collective-permute-start.1 = (bf16[32,128,128]{2,1,0:T(8,128)(2,1)S(1)}, bf16[32,128,128]{2,1,0:T(8,128)(2,1)}, u32[]{:S(2)}, u32[]{:S(2)}) collective-permute-start(bf16[32,128,128]{2,1,0:T(8,128)(2,1)S(1)} %convert_element_type.159), channel_id=1, source_target_pairs={{1,0},{2,1},{3,2},{4,3},{5,4},{6,5},{7,6},{8,7},{9,8},{10,9},{11,1... | collective-permute-start | bytes 3145736 | tf_op jit(solution)/shard_map/ppermute | solution.py:17
  16.6 19.4 %all-to-all-start = ((s32[16,1,64]{2,1,0:T(1,128)}), s32[16,1,64]{2,1,0:T(1,128)S(1)}, u32[]{:S(2)}, u32[]{:S(2)}) async-start(s32[16,1,64]{2,1,0:T(1,128)} %all_to_all.9), calls=%async_computation | async-start | bytes 16384 | tf_op jit(solution)/shard_map/all_to_all | solution.py:129
  35.9 6.5 %copy-start.7 = (f32[1,4]{1,0:T(1,128)S(1)}, f32[1,4]{1,0:T(1,128)}, u32[]{:S(2)}) copy-start(f32[1,4]{1,0:T(1,128)} %param.18) | copy-start | bytes 52
  35.9 6.5 %copy-start.8 = (f32[1,2]{1,0:T(1,128)S(1)}, f32[1,2]{1,0:T(1,128)}, u32[]{:S(2)}) copy-start(f32[1,2]{1,0:T(1,128)} %param.20) | copy-start | bytes 28
  35.9 6.6 %copy-start.9 = (f32[1,64]{1,0:T(1,128)S(1)}, f32[1,64]{1,0:T(1,128)}, u32[]{:S(2)}) copy-start(f32[1,64]{1,0:T(1,128)} %param.23) | copy-start | bytes 772
  35.9 7.2 %copy-start.10 = (f32[1,16]{1,0:T(1,128)S(1)}, f32[1,16]{1,0:T(1,128)}, u32[]{:S(2)}) copy-start(f32[1,16]{1,0:T(1,128)} %param.24) | copy-start | bytes 196
  35.9 9.1 %copy-start.6 = (s32[1,4]{1,0:T(1,128)S(1)}, s32[1,4]{1,0:T(1,128)}, u32[]{:S(2)}) copy-start(s32[1,4]{1,0:T(1,128)} %param.17) | copy-start | bytes 52
  35.9 9.1 %copy-start.5 = (s32[1,2]{1,0:T(1,128)S(1)}, s32[1,2]{1,0:T(1,128)}, u32[]{:S(2)}) copy-start(s32[1,2]{1,0:T(1,128)} %param.19) | copy-start | bytes 28
  36.0 9.7 %copy-start.11 = (f32[1,128]{1,0:T(1,128)S(1)}, f32[1,128]{1,0:T(1,128)}, u32[]{:S(2)}) copy-start(f32[1,128]{1,0:T(1,128)} %param.22) | copy-start | bytes 1540
  36.0 9.9 %copy-start.12 = (f32[1,16]{1,0:T(1,128)S(1)}, f32[1,16]{1,0:T(1,128)}, u32[]{:S(2)}) copy-start(f32[1,16]{1,0:T(1,128)} %param.25) | copy-start | bytes 196
  36.0 14.7 %copy-start.4 = (s32[1,128]{1,0:T(1,128)S(1)}, s32[1,128]{1,0:T(1,128)}, u32[]{:S(2)}) copy-start(s32[1,128]{1,0:T(1,128)} %param.21) | copy-start | bytes 1540
  36.0 60.1 %all-to-all-start.1 = ((bf16[16,64,8,128]{3,2,1,0:T(8,128)(2,1)}), bf16[16,64,8,128]{3,2,1,0:T(8,128)(2,1)S(1)}, u32[]{:S(2)}, u32[]{:S(2)}) async-start(bf16[16,64,8,128]{3,2,1,0:T(8,128)(2,1)} %bitcast.224), calls=%async_computation.1 | async-start | bytes 4194304 | tf_op jit(solution)/shard_map/all_to_all | solution.py:127
  42.2 214.1 %reduce-scatter.2.cloned.1.call-start = ((), (), s32[]{:S(2)}) async-start(), calls=%async_computation.3 | async-start | bytes 3145728 | tf_op jit(solution)/shard_map/reduce_scatter | solution.py:154
  130.1 27.6 %collective-permute-start.2 = (bf16[32,128,128]{2,1,0:T(8,128)(2,1)}, bf16[32,128,128]{2,1,0:T(8,128)(2,1)S(1)}, u32[]{:S(2)}, u32[]{:S(2)}) collective-permute-start(bf16[32,128,128]{2,1,0:T(8,128)(2,1)} %divide_convert_fusion), channel_id=1, source_target_pairs={{0,1},{1,2},{2,3},{3,4},{4,5},{5,6},{6,7},{7,8},{8,9},{9,10},{10,1... | collective-permute-start | bytes 3145736 | tf_op jit(solution)/shard_map/ppermute | solution.py:15
  132.1 25.5 %collective-permute-start.3 = (bf16[32,128,128]{2,1,0:T(8,128)(2,1)}, bf16[32,128,128]{2,1,0:T(8,128)(2,1)S(1)}, u32[]{:S(2)}, u32[]{:S(2)}) collective-permute-start(bf16[32,128,128]{2,1,0:T(8,128)(2,1)} %divide_convert_fusion), channel_id=1, source_target_pairs={{1,0},{2,1},{3,2},{4,3},{5,4},{6,5},{7,6},{8,7},{9,8},{10,9},{11,1... | collective-permute-start | bytes 3145736 | tf_op jit(solution)/shard_map/ppermute | solution.py:17
  201.5 54.8 %copy-start = (f32[32,128,128]{2,1,0:T(8,128)S(1)}, f32[32,128,128]{2,1,0:T(8,128)}, u32[]{:S(2)}) copy-start(f32[32,128,128]{2,1,0:T(8,128)} %param.13) | copy-start | bytes 6291460
Sparse Core Ops, SparseCore 0:
  224.1 32.1 reduce-scatter.1
where the time goes:
time: 269 us; the launch traced here: 265 us
  matrix products  135 us (50%)
  waiting for transfers between devices  63.3 us (24%)
  starting transfers between devices  24 us (9%)
  local copies, waits for them, and re-layouts  15.5 us (6%)
  between operations  13.8 us (5%)
  other arithmetic  13.5 us (5%)
    dot_general x2, matrix products, separable(): jnp.dot(table_z, padded_block.reshape(padded_block.shape[0], -1), preferr...  84.3 us
    dot_general x2, matrix products, separable(): jnp.dot(along_y.reshape(-1, out_shape[2]), table_x, preferred_element_typ...  44.3 us
    reduce_scatter x1, waiting for transfers between devices, shards(): lax.psum_scatter(correction, 'view', scatter_dimension=1, tiled=True)  32.3 us
    ppermute x2, waiting for transfers between devices, with_halo(): lax.ppermute(tail, axis, [(i, (i + 1) % count) for i in range(ends)])  21.8 us
    all_to_all x1, waiting for transfers between devices, shards(): lax.all_to_all(slot_positions, 'gz', split_axis=0, concat_axis=0, tiled=T...  9.13 us
    ppermute x2, starting transfers between devices, with_halo(): lax.ppermute(head, axis, [((i + 1) % count, i) for i in range(ends)])  7.37 us
    all_to_all x1, starting transfers between devices, shards(): lax.all_to_all(slot_positions, 'gz', split_axis=0, concat_axis=0, tiled=T...  6.24 us
    all_to_all x1, starting transfers between devices, shards(): lax.all_to_all(outgoing, 'gz', split_axis=0, concat_axis=0, tiled=True)  6.2 us
  transfers between devices with their start and end apart: 7, of which 3 were waited for; matrix products, arithmetic and copies ran while one was open for 22% of the time, Pallas kernels for 0%

commit v1 on v0

v1 whole, which is shorter than its diff:
```python
import functools

import jax
import jax.numpy as jnp
from jax import lax
from jax.experimental import pallas as pl
from jax.experimental.pallas import tpu as pltpu
from jax.sharding import PartitionSpec as P

BF16 = jnp.bfloat16
F32 = jnp.float32
CHUNKS = 4


def iota(shape, dim):
    return lax.broadcasted_iota(jnp.int32, shape, dim)


def tap_table(psf, count, which):
    total = psf[0, 0]
    for k in range(1, count):
        total = total + psf[0, k]
    table = jnp.zeros(which.shape, F32)
    for k in range(count):
        table = jnp.where(which == k, psf[0, k], table)
    return (table / jnp.full(which.shape, total, F32)).astype(BF16)


def small_weight(off, frac, column, source):
    fraction = jnp.full((1, 128), frac[0, column], F32)
    offset = jnp.full((1, 128), off[0, column], jnp.int32)
    low = (1.0 - fraction).astype(BF16).astype(F32)
    high = fraction.astype(BF16).astype(F32)
    return jnp.where(offset == source, low, 0.0) + jnp.where(offset + 1 == source, high, 0.0)


def step(
    dims,
    est, raw, slab, pos, off_z, frac_z, off_y, frac_y, off_x, frac_x, psf_z, psf_y, psf_x,
    out,
    pad1, pad2, work, blurred, joined, weights, mixed, outgoing, arrived, pos_out, pos_in, pos_row,
    placer, back, from_views, x_tables, slot_scr,
    halo_send, halo_recv, brick_send, brick_recv, pos_send, pos_recv, view_send, view_recv,
    xt_send, xt_recv, own_sem,
):
    planes, rows, cols, depth, height, bricks, n, nv, taps_z, taps_l = dims
    cells = depth * height
    wide = cells * cols
    cap = max(2, 2 * bricks // n)
    slots = n * cap
    block_planes = planes // depth
    block_rows = rows // height
    places = block_planes * block_rows
    half = taps_z // 2
    lat = taps_l // 2
    share = rows // nv
    part = rows // CHUNKS
    zpart = planes // CHUNKS
    me = lax.axis_index("gz")
    mv = lax.axis_index("view")

    barrier = pltpu.get_barrier_semaphore()

    @pl.loop(1, n)
    def _(i):
        pl.semaphore_signal(barrier, inc=1, device_id={"gz": lax.rem(me + i, n)})

    @pl.loop(1, nv)
    def _(i):
        pl.semaphore_signal(barrier, inc=1, device_id={"view": lax.rem(mv + i, nv)})

    def own_rows(source, pad):
        @pl.loop(0, rows, unroll=4)
        def _(y):
            pad[y, pl.ds(planes, planes), :] = source[pl.ds(y, planes, stride=rows), :].astype(BF16)

    own_rows(est, pad1)

    pl.semaphore_wait(barrier, n - 1 + nv - 1)

    def halo(pad, phase, to_right, c):
        peer = lax.rem(me + 1, n) if to_right else lax.rem(me + n - 1, n)
        side = 0 if to_right else 1
        return pltpu.make_async_remote_copy(
            src_ref=pad.at[pl.ds(c * part, part), pl.ds(planes, planes), :],
            dst_ref=pad.at[pl.ds(c * part, part), pl.ds(0 if to_right else 2 * planes, planes), :],
            send_sem=halo_send.at[phase, side, c],
            recv_sem=halo_recv.at[phase, side, c],
            device_id={"gz": peer},
            device_id_type=pl.DeviceIdType.MESH,
        )

    def halo_start(pad, phase, c):
        @pl.when(me < n - 1)
        def _():
            halo(pad, phase, True, c).start()

        @pl.when(me > 0)
        def _():
            halo(pad, phase, False, c).start()

    def halo_wait(pad, phase, c):
        @pl.when(me > 0)
        def _():
            halo(pad, phase, True, c).wait_recv()

        @pl.when(me < n - 1)
        def _():
            halo(pad, phase, False, c).wait_recv()

    def halo_sent(pad, phase, c):
        @pl.when(me < n - 1)
        def _():
            halo(pad, phase, True, c).wait_send()

        @pl.when(me > 0)
        def _():
            halo(pad, phase, False, c).wait_send()

    for c in range(CHUNKS):
        halo_start(pad1, 0, c)

    @pl.when(me == 0)
    def _():
        for pad in (pad1, pad2):
            pad[:, pl.ds(0, planes), :] = jnp.zeros((rows, planes, cols), BF16)

    @pl.when(me == n - 1)
    def _():
        for pad in (pad1, pad2):
            pad[:, pl.ds(2 * planes, planes), :] = jnp.zeros((rows, planes, cols), BF16)

    source = iota((cols, cols), 0)
    low = (1.0 - frac_x[...]).astype(BF16).astype(F32)
    high = frac_x[...].astype(BF16).astype(F32)
    along = jnp.where(source == off_x[...], low, 0.0) + jnp.where(source == off_x[...] + 1, high, 0.0)
    for a in range(depth):
        for c in range(depth):
            wz = small_weight(off_z, frac_z, c, a)
            for e in range(height):
                for d in range(height):
                    wy = small_weight(off_y, frac_y, d, e)
                    wzy = (wz * wy).astype(BF16).astype(F32)
                    weights[
                        (a * height + e) * cols:(a * height + e + 1) * cols,
                        (c * height + d) * cols:(c * height + d + 1) * cols,
                    ] = (along * wzy).astype(BF16)
    for i in range(wide // 256):
        mixed[:, i * 256:(i + 1) * 256] = jnp.dot(
            raw[...], weights[:, i * 256:(i + 1) * 256], preferred_element_type=F32
        ).astype(BF16)

    slab_v = slab[...]
    member = iota((n, bricks), 0) == slab_v
    before = (iota((bricks, bricks), 0) < iota((bricks, bricks), 1)).astype(F32).astype(BF16)
    earlier = jnp.dot(member.astype(F32).astype(BF16), before, preferred_element_type=F32)
    order = jnp.sum(jnp.where(member, earlier, 0.0), axis=0, keepdims=True).astype(jnp.int32)
    slot_scr[...] = slab_v * cap + order
    pos_v = pos[...]
    row16 = iota((16, bricks), 0)
    pos_pair = jnp.where(
        row16 == 0, pos_v // 64 + 1, jnp.where(row16 == 1, lax.rem(pos_v, 64), 0)
    ).astype(F32).astype(BF16)
    for i in range(slots // 256):
        chosen = ((iota((256, bricks), 0) + i * 256) == slot_scr[...]).astype(F32).astype(BF16)
        outgoing[i * 256:(i + 1) * 256, :] = jnp.dot(
            chosen, mixed[...], preferred_element_type=F32
        ).astype(BF16)
        slot_pos = lax.dot_general(
            pos_pair, chosen, (((1,), (1,)), ((), ())), preferred_element_type=F32
        )
        for j in range(256 // cap):
            pos_out[i * (256 // cap) + j, :, 0:cap] = slot_pos[:, j * cap:(j + 1) * cap].astype(BF16)

    def brick_copy(peer, owner):
        return pltpu.make_async_remote_copy(
            src_ref=outgoing.at[pl.ds(pl.multiple_of(peer * cap, cap), cap), :],
            dst_ref=arrived.at[pl.ds(pl.multiple_of(owner * cap, cap), cap), :],
            send_sem=brick_send.at[peer],
            recv_sem=brick_recv.at[owner],
            device_id={"gz": peer},
            device_id_type=pl.DeviceIdType.MESH,
        )

    def pos_copy(peer, owner):
        return pltpu.make_async_remote_copy(
            src_ref=pos_out.at[peer],
            dst_ref=pos_in.at[owner],
            send_sem=pos_send.at[peer],
            recv_sem=pos_recv.at[owner],
            device_id={"gz": peer},
            device_id_type=pl.DeviceIdType.MESH,
        )

    @pl.loop(1, n)
    def _(i):
        peer = lax.rem(me + i, n)
        brick_copy(peer, me).start()
        pos_copy(peer, me).start()

    mine = pl.ds(pl.multiple_of(me * cap, cap), cap)
    own_bricks = pltpu.make_async_copy(outgoing.at[mine, :], arrived.at[mine, :], own_sem.at[0])
    own_pos = pltpu.make_async_copy(pos_out.at[me], pos_in.at[me], own_sem.at[1])
    own_bricks.start()
    own_pos.start()

    def true_row(r):
        return lax.rem(r, block_rows) * height + r // block_rows

    ii, jj = iota((rows, rows), 0), iota((rows, rows), 1)
    fy = tap_table(psf_y, taps_l, jj - true_row(ii) + lat)
    by = tap_table(psf_y, taps_l, ii - true_row(jj) + lat)
    ci, cj = iota((cols, cols), 0), iota((cols, cols), 1)
    fx = tap_table(psf_x, taps_l, ci - cj + lat)
    x_tables[mv] = tap_table(psf_x, taps_l, cj - ci + lat)
    zi, zj = iota((planes, 3 * planes), 0), iota((planes, 3 * planes), 1)
    fz = tap_table(psf_z, taps_z, zj - zi - (planes - half))
    bz = tap_table(psf_z, taps_z, planes + half + zi - zj)

    def xt_copy(peer, owner):
        return pltpu.make_async_remote_copy(
            src_ref=x_tables.at[mv],
            dst_ref=x_tables.at[owner],
            send_sem=xt_send.at[peer],
            recv_sem=xt_recv.at[owner],
            device_id={"view": peer},
            device_id_type=pl.DeviceIdType.MESH,
        )

    @pl.loop(1, nv)
    def _(i):
        xt_copy(lax.rem(mv + i, nv), mv).start()

    def z_pass(pad, table, c):
        @pl.loop(0, part // 4, unroll=2)
        def _(i):
            y = c * part + i * 4
            block = jnp.concatenate([pad[y + j] for j in range(4)], axis=1)
            result = jnp.dot(table, block, preferred_element_type=F32)
            result = result.astype(BF16).astype(F32)
            for j in range(4):
                work[pl.ds((y + j) * planes, planes), :] = result[:, j * cols:(j + 1) * cols]

    def y_pass(table, z):
        block = jnp.concatenate(
            [work[pl.ds(z + j, rows, stride=planes), :].astype(BF16) for j in range(2)], axis=1
        )
        return jnp.dot(table, block, preferred_element_type=F32).astype(BF16)

    for c in range(CHUNKS):
        halo_wait(pad1, 0, c)
        z_pass(pad1, fz, c)

    @pl.loop(0, planes // 2, unroll=2)
    def _(i):
        along_y = y_pass(fy, 2 * i)
        for j in range(2):
            blurred[2 * i + j] = jnp.dot(
                along_y[:, j * cols:(j + 1) * cols], fx, preferred_element_type=F32
            )

    own_pos.wait()

    @pl.loop(1, n)
    def _(i):
        pos_copy(me, lax.rem(me + n - i, n)).wait_recv()

    for s in range(n):
        pair = pos_in[s].astype(F32)
        pos_row[0:1, s * cap:(s + 1) * cap] = ((pair[0:1] - 1.0) * 64.0 + pair[1:2])[:, 0:cap]
    for i in range(places // 128):
        place = (iota((128, slots), 0) + i * 128).astype(F32)
        placer[i * 128:(i + 1) * 128, :] = (place == pos_row[0:1, :]).astype(F32).astype(BF16)

    own_bricks.wait()

    @pl.loop(1, n)
    def _(i):
        brick_copy(me, lax.rem(me + n - i, n)).wait_recv()

    for c in range(depth):
        for d in range(height):
            at = (c * height + d) * cols
            if d % 2 == 0:
                added = jnp.dot(placer[...], arrived[:, at:at + 2 * cols], preferred_element_type=F32)
            joined[:, c, d, :, :] = added[:, (d % 2) * cols:(d % 2 + 1) * cols].reshape(
                block_planes, block_rows, cols
            )

    @pl.loop(0, block_planes)
    def _(i):
        for c in range(depth):
            z = i * depth + c
            for d in range(height):
                work[pl.ds(z * rows + d * block_rows, block_rows), :] = (
                    1.0 + joined[i, c, d]
                ) / blurred[z, d * block_rows:(d + 1) * block_rows, :]

    own_rows(work, pad2)
    for c in range(CHUNKS):
        halo_start(pad2, 1, c)
    for c in range(CHUNKS):
        halo_wait(pad2, 1, c)
        z_pass(pad2, bz, c)

    def view_copy(peer, owner, c):
        return pltpu.make_async_remote_copy(
            src_ref=back.at[pl.ds(c * zpart, zpart), pl.ds(pl.multiple_of(peer * share, share), share), :],
            dst_ref=from_views.at[owner, pl.ds(c * zpart, zpart), :, :],
            send_sem=view_send.at[peer, c],
            recv_sem=view_recv.at[owner, c],
            device_id={"view": peer},
            device_id_type=pl.DeviceIdType.MESH,
        )

    for c in range(CHUNKS):
        @pl.loop(0, zpart // 2, unroll=2)
        def _(i):
            z = c * zpart + 2 * i
            along_y = y_pass(by, z)
            for j in range(2):
                back[z + j] = along_y[:, j * cols:(j + 1) * cols]

        @pl.loop(1, nv)
        def _(i):
            view_copy(lax.rem(mv + i, nv), mv, c).start()

    first = pl.multiple_of(mv * share, share)

    @pl.loop(0, planes)
    def _(z):
        out[z] = jnp.dot(
            back[z, pl.ds(first, share), :], x_tables[mv], preferred_element_type=F32
        )

    @pl.loop(1, nv)
    def _(i):
        xt_copy(mv, lax.rem(mv + i, nv)).wait_recv()

    for c in range(CHUNKS):
        @pl.loop(1, nv)
        def _(i):
            view_copy(mv, lax.rem(mv + i, nv), c).wait_recv()

        @pl.loop(0, zpart)
        def _(i):
            z = c * zpart + i
            total = out[z]
            for v in range(1, nv):
                other = lax.rem(mv + v, nv)
                total = total + jnp.dot(
                    from_views[other, z], x_tables[other], preferred_element_type=F32
                )
            out[z] = est[pl.ds(pl.multiple_of(z * rows + first, share), share), :] * total * (1.0 / nv)

    for c in range(CHUNKS):
        halo_sent(pad1, 0, c)
        halo_sent(pad2, 1, c)

        @pl.loop(1, nv)
        def _(i):
            view_copy(lax.rem(mv + i, nv), mv, c).wait_send()

    @pl.loop(1, nv)
    def _(i):
        xt_copy(lax.rem(mv + i, nv), mv).wait_send()

    @pl.loop(1, n)
    def _(i):
        peer = lax.rem(me + i, n)
        brick_copy(peer, me).wait_send()
        pos_copy(peer, me).wait_send()


def shards(
    estimate, raw_bricks, brick_slab, brick_pos, off_z, frac_z, off_y, frac_y, off_x, frac_x,
    psf_z, psf_y, psf_x,
):
    planes, rows, cols = estimate.shape
    _, bricks, depth, height, _ = raw_bricks.shape
    n, nv = lax.axis_size("gz"), lax.axis_size("view")
    taps_z, taps_l = psf_z.shape[1], psf_x.shape[1]
    cells = depth * height
    wide = cells * cols
    cap = max(2, 2 * bricks // n)
    slots = n * cap
    share = rows // nv
    block_planes, block_rows = planes // depth, rows // height
    places = block_planes * block_rows
    dims = (planes, rows, cols, depth, height, bricks, n, nv, taps_z, taps_l)
    vmem = pl.BlockSpec(memory_space=pltpu.VMEM)
    smem = pl.BlockSpec(memory_space=pltpu.SMEM)
    dma = pltpu.SemaphoreType.DMA
    return pl.pallas_call(
        functools.partial(step, dims),
        out_shape=jax.ShapeDtypeStruct((planes, share, cols), F32),
        in_specs=[vmem] * 4 + [smem] * 4 + [vmem] * 2 + [smem] * 3,
        out_specs=vmem,
        scratch_shapes=[
            pltpu.VMEM((rows, 3 * planes, cols), BF16),
            pltpu.VMEM((rows, 3 * planes, cols), BF16),
            pltpu.VMEM((rows * planes, cols), F32),
            pltpu.VMEM((planes, rows, cols), F32),
            pltpu.VMEM((block_planes, depth, height, block_rows, cols), F32),
            pltpu.VMEM((wide, wide), BF16),
            pltpu.VMEM((bricks, wide), BF16),
            pltpu.VMEM((slots, wide), BF16),
            pltpu.VMEM((slots, wide), BF16),
            pltpu.VMEM((n, 16, 128), BF16),
            pltpu.VMEM((n, 16, 128), BF16),
            pltpu.VMEM((8, slots), F32),
            pltpu.VMEM((places, slots), BF16),
            pltpu.VMEM((planes, rows, cols), BF16),
            pltpu.VMEM((nv, planes, share, cols), BF16),
            pltpu.VMEM((nv, cols, cols), BF16),
            pltpu.VMEM((1, bricks), jnp.int32),
            dma((2, 2, CHUNKS)),
            dma((2, 2, CHUNKS)),
            dma((n,)),
            dma((n,)),
            dma((n,)),
            dma((n,)),
            dma((nv, CHUNKS)),
            dma((nv, CHUNKS)),
            dma((nv,)),
            dma((nv,)),
            dma((2,)),
        ],
        compiler_params=pltpu.CompilerParams(
            collective_id=0, has_side_effects=True, vmem_limit_bytes=48 * 1024 * 1024
        ),
    )(
        estimate.reshape(planes * rows, cols),
        raw_bricks.reshape(bricks, wide),
        brick_slab.reshape(1, bricks),
        brick_pos,
        off_z, frac_z, off_y, frac_y, off_x, frac_x, psf_z, psf_y, psf_x,
    )


def solution(mesh):
    in_specs = (
        P("gz", None, None),
        P("view", "gz", None, None, None),
        P("view", "gz", None),
        P("view", "gz"),
    ) + (P("view", None),) * 9
    out_specs = P("gz", "view", None)
    return jax.shard_map(shards, mesh=mesh, in_specs=in_specs, out_specs=out_specs, check_vma=False)
```

time: 269 us -> 108 us (0.40)
  matrix products: 135 us -> 0 us
  Pallas kernels: 0 us -> 99.3 us
  waiting for transfers between devices: 63.3 us -> 0 us
  starting transfers between devices: 24 us -> 0 us
  between operations: 13.8 us -> 0.09 us
  other arithmetic: 13.5 us -> 0 us
  local copies, waits for them, and re-layouts: 15.5 us -> 7.54 us
    dot_general x7 -> x0, matrix products: 135 us -> none  [the longest x2 84.3 us: separable(): jnp.dot(table_z, padded_block.reshape(padded_block.shape[0], -1), preferr...]
    pallas_call x0 -> x1, Pallas kernels: none -> 99.3 us  [shards(): pl.pallas_call(functools.partial(step, dims), out_shape=jax.ShapeDtypeStr...]
    reduce_scatter x1 -> x0, waiting for transfers between devices: 32.3 us -> none  [shards(): lax.psum_scatter(correction, 'view', scatter_dimension=1, tiled=True)]
    ppermute x4 -> x0, waiting for transfers between devices: 21.8 us -> none  [the longest x2 21.8 us: with_halo(): lax.ppermute(tail, axis, [(i, (i + 1) % count) for i in range(ends)])]
    all_to_all x2 -> x0, starting transfers between devices: 12.4 us -> none  [the longest x1 6.24 us: shards(): lax.all_to_all(slot_positions, 'gz', split_axis=0, concat_axis=0, tiled=T...]
    ppermute x4 -> x0, starting transfers between devices: 11.3 us -> none  [the longest x2 7.37 us: with_halo(): lax.ppermute(head, axis, [((i + 1) % count, i) for i in range(ends)])]
    all_to_all x2 -> x0, waiting for transfers between devices: 9.13 us -> none  [the longest x1 9.13 us: shards(): lax.all_to_all(slot_positions, 'gz', split_axis=0, concat_axis=0, tiled=T...]
    slice x7 -> x0, local copies, waits for them, and re-layouts: 4.46 us -> none  [the longest x6 4.24 us: band_table(): normed[tap_index]]
  transfers between devices with their start and end apart: 7 -> 0, of which waited for: 3 -> 0; matrix products, arithmetic and copies ran while one was open for 22% -> 0% of each run, Pallas kernels for 0% -> 0%
where the time goes in v1:
time: 108 us; the launch traced here: 107 us
  Pallas kernels  99.3 us (92%)
  local copies, waits for them, and re-layouts  7.54 us (7%)
    pallas_call x1, Pallas kernels, shards(): pl.pallas_call(functools.partial(step, dims), out_shape=jax.ShapeDtypeStr...  99.3 us
    unnamed x25, local copies, waits for them, and re-layouts  5.6 us

profile of v1, /device:TPU:12, one launch (start us, length us, event | category | flops | bytes accessed | tf_op | source)
XLA Modules:
  0.0 107.0 jit_solution(1585636969420365092)
XLA Ops:
  0.0 0.0 copy-start.5
  0.0 0.0 copy-start.4
  0.0 0.0 copy-start.3
  0.0 0.0 copy-start.1
  0.0 0.0 copy-start
  0.0 1.9 %reshape.10.raw = bf16[512,1024]{1,0:T(8,128)(2,1)S(1)} reshape(bf16[1,512,4,2,128]{4,3,2,1,0:T(2,128)(2,1)} %param.14) | data formatting | bytes 2097152 | tf_op jit(solution)/shard_map/reshape | solution.py:434
  2.0 0.0 copy-done.5
  2.0 0.0 copy-done.4
  2.0 0.0 copy-done.3
  2.0 0.0 copy-done.1
  2.0 0.0 copy-done
  2.0 0.0 copy-start.2
  2.0 0.7 copy-done.2
  2.7 0.0 copy-start.6
  2.7 0.7 copy-done.6
  3.4 0.0 copy-start.7
  3.4 0.7 copy-done.7
  4.0 0.0 copy-start.8
  4.0 0.7 copy-done.8
  4.7 0.0 copy-start.9
  4.7 0.7 copy-done.9
  5.3 0.0 copy-start.10
  5.3 0.7 copy-done.10
  6.0 0.0 copy-start.11
  6.0 0.7 copy-done.11
  6.6 99.3 %shard_map.127 = f32[32,64,128]{2,1,0:T(8,128)S(1)} custom-call(f32[4096,128]{1,0:T(8,128)S(1)} %bitcast.2, bf16[512,1024]{1,0:T(8,128)(2,1)S(1)} %reshape.10.raw, s32[1,512]{1,0:T(1,128)S(1)} %bitcast.3, s32[1,512]{1,0:T(1,128)S(1)} %copy-done.2, s32[1,4]{1,0:T(1,128)S(1)} %copy-done.3, f32[1,4]{1,0:T(1,128)S(1)} %copy-done.4, s32[1,2]{1,0:T(1,128)S(1)} %copy-done.5, ...), custom_call_target="tpu_custom_call" | custom-call | tf_op jit(solution)/shard_map/pallas_call | solution.py:394
  106.0 1.0 copy.15
Async XLA Ops:
  0.0 2.0 %copy-start.5 = (s32[1,2]{1,0:T(1,128)S(1)}, s32[1,2]{1,0:T(1,128)}, u32[]{:S(2)}) copy-start(s32[1,2]{1,0:T(1,128)} %off_y.1) | copy-start | bytes 28
  0.0 2.0 %copy-start.4 = (f32[1,4]{1,0:T(1,128)S(1)}, f32[1,4]{1,0:T(1,128)}, u32[]{:S(2)}) copy-start(f32[1,4]{1,0:T(1,128)} %frac_z.1) | copy-start | bytes 52
  0.0 2.0 %copy-start.3 = (s32[1,4]{1,0:T(1,128)S(1)}, s32[1,4]{1,0:T(1,128)}, u32[]{:S(2)}) copy-start(s32[1,4]{1,0:T(1,128)} %off_z.1) | copy-start | bytes 52
  0.0 2.0 %copy-start.1 = (s32[1,512,1]{1,2,0:T(1,128)S(1)}, s32[1,512,1]{1,2,0:T(1,128)}, u32[]{:S(2)}) copy-start(s32[1,512,1]{1,2,0:T(1,128)} %param.15) | copy-start | bytes 6148
  0.0 2.0 %copy-start = (f32[32,128,128]{2,1,0:T(8,128)S(1)}, f32[32,128,128]{2,1,0:T(8,128)}, u32[]{:S(2)}) copy-start(f32[32,128,128]{2,1,0:T(8,128)} %param.13) | copy-start | bytes 6291460
  2.0 0.7 copy-start.2
  2.7 0.7 copy-start.6
  3.4 0.7 copy-start.7
  4.0 0.7 copy-start.8
  4.7 0.7 copy-start.9
  5.3 0.7 copy-start.10
  6.0 0.7 copy-start.11

commit v2 on v1

--- a/solution.py
+++ b/solution.py
@@ -17,18 +17,16 @@
 
 
 def tap_table(psf, count, which):
-    total = psf[0, 0]
-    for k in range(1, count):
-        total = total + psf[0, k]
+    normed = psf[...] / jnp.sum(psf[...], axis=1, keepdims=True)
     table = jnp.zeros(which.shape, F32)
     for k in range(count):
-        table = jnp.where(which == k, psf[0, k], table)
-    return (table / jnp.full(which.shape, total, F32)).astype(BF16)
+        table = jnp.where(which == k, jnp.broadcast_to(normed[0:1, k:k + 1], which.shape), table)
+    return table.astype(BF16)
 
 
 def small_weight(off, frac, column, source):
-    fraction = jnp.full((1, 128), frac[0, column], F32)
-    offset = jnp.full((1, 128), off[0, column], jnp.int32)
+    fraction = jnp.broadcast_to(frac[0:1, column:column + 1], (1, 128))
+    offset = jnp.broadcast_to(off[0:1, column:column + 1], (1, 128))
     low = (1.0 - fraction).astype(BF16).astype(F32)
     high = fraction.astype(BF16).astype(F32)
     return jnp.where(offset == source, low, 0.0) + jnp.where(offset + 1 == source, high, 0.0)
@@ -38,9 +36,9 @@
     dims,
     est, raw, slab, pos, off_z, frac_z, off_y, frac_y, off_x, frac_x, psf_z, psf_y, psf_x,
     out,
-    pad1, pad2, work, blurred, joined, weights, mixed, outgoing, arrived, pos_out, pos_in, pos_row,
+    pad1, pad2, work, blurred, joined, weights, by_cell, mixed, outgoing, arrived, pos_out, pos_in, pos_row,
     placer, back, from_views, x_tables, slot_scr,
-    halo_send, halo_recv, brick_send, brick_recv, pos_send, pos_recv, view_send, view_recv,
+    halo_send, halo_recv, share_send, share_recv, pass_send, pass_recv, brick_send, brick_recv, pos_send, pos_recv, view_send, view_recv,
     xt_send, xt_recv, own_sem,
 ):
     planes, rows, cols, depth, height, bricks, n, nv, taps_z, taps_l = dims
@@ -56,6 +54,7 @@
     share = rows // nv
     part = rows // CHUNKS
     zpart = planes // CHUNKS
+    piece = share // 2
     me = lax.axis_index("gz")
     mv = lax.axis_index("view")
 
@@ -69,56 +68,60 @@
     def _(i):
         pl.semaphore_signal(barrier, inc=1, device_id={"view": lax.rem(mv + i, nv)})
 
-    def own_rows(source, pad):
-        @pl.loop(0, rows, unroll=4)
-        def _(y):
+    def own_rows(source, pad, start, count):
+        @pl.loop(0, count, unroll=8)
+        def _(i):
+            y = start + i
             pad[y, pl.ds(planes, planes), :] = source[pl.ds(y, planes, stride=rows), :].astype(BF16)
 
-    own_rows(est, pad1)
+    own_rows(est, pad1, 0, rows)
 
     pl.semaphore_wait(barrier, n - 1 + nv - 1)
 
-    def halo(pad, phase, to_right, c):
-        peer = lax.rem(me + 1, n) if to_right else lax.rem(me + n - 1, n)
-        side = 0 if to_right else 1
+    left, right = lax.rem(me + n - 1, n), lax.rem(me + 1, n)
+
+    def neighbours(start_row, count, pad, send_sems, recv_sems, c):
+        def copy(side):
+            return pltpu.make_async_remote_copy(
+                src_ref=pad.at[pl.ds(start_row, count), pl.ds(planes, planes), :],
+                dst_ref=pad.at[pl.ds(start_row, count), pl.ds(side * 2 * planes, planes), :],
+                send_sem=send_sems.at[side, c],
+                recv_sem=recv_sems.at[side, c],
+                device_id={"gz": (right, left)[side]},
+                device_id_type=pl.DeviceIdType.MESH,
+            )
+
+        return copy
+
+    def on_sides(to_right, to_left, arriving=False):
+        @pl.when(me > 0 if arriving else me < n - 1)
+        def _():
+            to_right()
+
+        @pl.when(me < n - 1 if arriving else me > 0)
+        def _():
+            to_left()
+
+    def share_copy(c):
+        return neighbours(mv * share + c * piece, piece, pad1, share_send, share_recv, c)
+
+    def pass_copy(side, c, peer, owner):
+        block = pad1.at[pl.ds(owner * share + c * piece, piece), pl.ds(side * 2 * planes, planes), :]
         return pltpu.make_async_remote_copy(
-            src_ref=pad.at[pl.ds(c * part, part), pl.ds(planes, planes), :],
-            dst_ref=pad.at[pl.ds(c * part, part), pl.ds(0 if to_right else 2 * planes, planes), :],
-            send_sem=halo_send.at[phase, side, c],
-            recv_sem=halo_recv.at[phase, side, c],
-            device_id={"gz": peer},
+            src_ref=block,
+            dst_ref=block,
+            send_sem=pass_send.at[peer, side, c],
+            recv_sem=pass_recv.at[owner, side, c],
+            device_id={"view": peer},
             device_id_type=pl.DeviceIdType.MESH,
         )
 
-    def halo_start(pad, phase, c):
-        @pl.when(me < n - 1)
-        def _():
-            halo(pad, phase, True, c).start()
-
-        @pl.when(me > 0)
-        def _():
-            halo(pad, phase, False, c).start()
-
-    def halo_wait(pad, phase, c):
-        @pl.when(me > 0)
-        def _():
-            halo(pad, phase, True, c).wait_recv()
-
-        @pl.when(me < n - 1)
-        def _():
-            halo(pad, phase, False, c).wait_recv()
-
-    def halo_sent(pad, phase, c):
-        @pl.when(me < n - 1)
-        def _():
-            halo(pad, phase, True, c).wait_send()
-
-        @pl.when(me > 0)
-        def _():
-            halo(pad, phase, False, c).wait_send()
-
-    for c in range(CHUNKS):
-        halo_start(pad1, 0, c)
+    def halo(c):
+        return neighbours(c * part, part, pad2, halo_send, halo_recv, c)
+
+    for c in range(2):
+        copy = share_copy(c)
+        on_sides(copy(0).start, copy(1).start)
 
     @pl.when(me == 0)
     def _():
@@ -134,20 +137,28 @@
     low = (1.0 - frac_x[...]).astype(BF16).astype(F32)
     high = frac_x[...].astype(BF16).astype(F32)
     along = jnp.where(source == off_x[...], low, 0.0) + jnp.where(source == off_x[...] + 1, high, 0.0)
+    along_b = along.astype(BF16)
+    quarter = bricks * cells // 4
+    for i in range(4):
+        work[i * quarter:(i + 1) * quarter, :] = jnp.dot(
+            raw[i * quarter:(i + 1) * quarter, :], along_b, preferred_element_type=F32
+        ).astype(BF16).astype(F32)
+    for q in range(cells):
+        by_cell[:, q * cols:(q + 1) * cols] = work[pl.ds(q, bricks, stride=cells), :].astype(BF16)
+    unit = (iota((cols, cols), 0) == iota((cols, cols), 1)).astype(F32)
     for a in range(depth):
         for c in range(depth):
             wz = small_weight(off_z, frac_z, c, a)
             for e in range(height):
                 for d in range(height):
                     wy = small_weight(off_y, frac_y, d, e)
-                    wzy = (wz * wy).astype(BF16).astype(F32)
                     weights[
                         (a * height + e) * cols:(a * height + e + 1) * cols,
                         (c * height + d) * cols:(c * height + d + 1) * cols,
-                    ] = (along * wzy).astype(BF16)
+                    ] = (unit * (wz * wy)).astype(BF16)
     for i in range(wide // 256):
         mixed[:, i * 256:(i + 1) * 256] = jnp.dot(
-            raw[...], weights[:, i * 256:(i + 1) * 256], preferred_element_type=F32
+            by_cell[...], weights[:, i * 256:(i + 1) * 256], preferred_element_type=F32
         ).astype(BF16)
 
     slab_v = slab[...]
@@ -231,10 +242,10 @@
     def _(i):
         xt_copy(lax.rem(mv + i, nv), mv).start()
 
-    def z_pass(pad, table, c):
-        @pl.loop(0, part // 4, unroll=2)
-        def _(i):
-            y = c * part + i * 4
+    def z_pass(pad, table, start, count):
+        @pl.loop(0, count // 4, unroll=4)
+        def _(i):
+            y = start + i * 4
             block = jnp.concatenate([pad[y + j] for j in range(4)], axis=1)
             result = jnp.dot(table, block, preferred_element_type=F32)
             result = result.astype(BF16).astype(F32)
@@ -247,11 +258,31 @@
         )
         return jnp.dot(table, block, preferred_element_type=F32).astype(BF16)
 
-    for c in range(CHUNKS):
-        halo_wait(pad1, 0, c)
-        z_pass(pad1, fz, c)
-
-    @pl.loop(0, planes // 2, unroll=2)
+    def pass_on(side, c):
+        @pl.loop(1, nv)
+        def _(i):
+            pass_copy(side, c, lax.rem(mv + i, nv), mv).start()
+
+    def pass_take(side, c, owner):
+        pass_copy(side, c, mv, owner).wait_recv()
+
+    def pass_sent(side, c):
+        @pl.loop(1, nv)
+        def _(i):
+            pass_copy(side, c, lax.rem(mv + i, nv), mv).wait_send()
+
+    for c in range(2):
+        copy = share_copy(c)
+        on_sides(copy(0).wait_recv, copy(1).wait_recv, arriving=True)
+        on_sides(lambda: pass_on(0, c), lambda: pass_on(1, c), arriving=True)
+    z_pass(pad1, fz, mv * share, share)
+    for v in range(1, nv):
+        owner = lax.rem(mv + nv - v, nv)
+        for c in range(2):
+            on_sides(lambda: pass_take(0, c, owner), lambda: pass_take(1, c, owner), arriving=True)
+            z_pass(pad1, fz, owner * share + c * piece, piece)
+
+    @pl.loop(0, planes // 2, unroll=4)
     def _(i):
         along_y = y_pass(fy, 2 * i)
         for j in range(2):
@@ -287,21 +318,24 @@
                 block_planes, block_rows, cols
             )
 
-    @pl.loop(0, block_planes)
-    def _(i):
-        for c in range(depth):
-            z = i * depth + c
-            for d in range(height):
-                work[pl.ds(z * rows + d * block_rows, block_rows), :] = (
-                    1.0 + joined[i, c, d]
-                ) / blurred[z, d * block_rows:(d + 1) * block_rows, :]
-
-    own_rows(work, pad2)
     for c in range(CHUNKS):
-        halo_start(pad2, 1, c)
+        d, at_row = c * part // block_rows, c * part % block_rows
+
+        @pl.loop(0, block_planes)
+        def _(i):
+            for k in range(depth):
+                z = i * depth + k
+                work[pl.ds(z * rows + c * part, part), :] = (
+                    1.0 + joined[i, k, d, at_row:at_row + part, :]
+                ) / blurred[z, c * part:(c + 1) * part, :]
+
+        own_rows(work, pad2, c * part, part)
+        copy = halo(c)
+        on_sides(copy(0).start, copy(1).start)
     for c in range(CHUNKS):
-        halo_wait(pad2, 1, c)
-        z_pass(pad2, bz, c)
+        copy = halo(c)
+        on_sides(copy(0).wait_recv, copy(1).wait_recv, arriving=True)
+        z_pass(pad2, bz, c * part, part)
 
     def view_copy(peer, owner, c):
         return pltpu.make_async_remote_copy(
@@ -314,7 +348,7 @@
         )
 
     for c in range(CHUNKS):
-        @pl.loop(0, zpart // 2, unroll=2)
+        @pl.loop(0, zpart // 2, unroll=4)
         def _(i):
             z = c * zpart + 2 * i
             along_y = y_pass(by, z)
@@ -327,12 +361,6 @@
 
     first = pl.multiple_of(mv * share, share)
 
-    @pl.loop(0, planes)
-    def _(z):
-        out[z] = jnp.dot(
-            back[z, pl.ds(first, share), :], x_tables[mv], preferred_element_type=F32
-        )
-
     @pl.loop(1, nv)
     def _(i):
         xt_copy(mv, lax.rem(mv + i, nv)).wait_recv()
@@ -342,20 +370,34 @@
         def _(i):
             view_copy(mv, lax.rem(mv + i, nv), c).wait_recv()
 
-        @pl.loop(0, zpart)
-        def _(i):
-            z = c * zpart + i
-            total = out[z]
-            for v in range(1, nv):
-                other = lax.rem(mv + v, nv)
-                total = total + jnp.dot(
-                    from_views[other, z], x_tables[other], preferred_element_type=F32
-                )
-            out[z] = est[pl.ds(pl.multiple_of(z * rows + first, share), share), :] * total * (1.0 / nv)
-
+        planes_c = slice(c * zpart, (c + 1) * zpart)
+        total = jnp.dot(
+            back[planes_c, pl.ds(first, share), :].reshape(zpart * share, cols),
+            x_tables[mv],
+            preferred_element_type=F32,
+        )
+        for v in range(1, nv):
+            other = lax.rem(mv + v, nv)
+            total = total + jnp.dot(
+                from_views[other, planes_c].reshape(zpart * share, cols),
+                x_tables[other],
+                preferred_element_type=F32,
+            )
+        for k in range(zpart):
+            z = c * zpart + k
+            out[z] = (
+                est[pl.ds(pl.multiple_of(z * rows + first, share), share), :]
+                * total[k * share:(k + 1) * share]
+                * (1.0 / nv)
+            )
+
+    for c in range(2):
+        copy = share_copy(c)
+        on_sides(copy(0).wait_send, copy(1).wait_send)
+        on_sides(lambda: pass_sent(0, c), lambda: pass_sent(1, c), arriving=True)
     for c in range(CHUNKS):
-        halo_sent(pad1, 0, c)
-        halo_sent(pad2, 1, c)
+        copy = halo(c)
+        on_sides(copy(0).wait_send, copy(1).wait_send)
 
         @pl.loop(1, nv)
         def _(i):
@@ -389,20 +431,20 @@
     places = block_planes * block_rows
     dims = (planes, rows, cols, depth, height, bricks, n, nv, taps_z, taps_l)
     vmem = pl.BlockSpec(memory_space=pltpu.VMEM)
-    smem = pl.BlockSpec(memory_space=pltpu.SMEM)
     dma = pltpu.SemaphoreType.DMA
     return pl.pallas_call(
         functools.partial(step, dims),
         out_shape=jax.ShapeDtypeStruct((planes, share, cols), F32),
-        in_specs=[vmem] * 4 + [smem] * 4 + [vmem] * 2 + [smem] * 3,
+        in_specs=[vmem] * 13,
         out_specs=vmem,
         scratch_shapes=[
             pltpu.VMEM((rows, 3 * planes, cols), BF16),
             pltpu.VMEM((rows, 3 * planes, cols), BF16),
-            pltpu.VMEM((rows * planes, cols), F32),
+            pltpu.VMEM((max(rows * planes, bricks * cells), cols), F32),
             pltpu.VMEM((planes, rows, cols), F32),
             pltpu.VMEM((block_planes, depth, height, block_rows, cols), F32),
             pltpu.VMEM((wide, wide), BF16),
+            pltpu.VMEM((bricks, wide), BF16),
             pltpu.VMEM((bricks, wide), BF16),
             pltpu.VMEM((slots, wide), BF16),
             pltpu.VMEM((slots, wide), BF16),
@@ -414,8 +456,12 @@
             pltpu.VMEM((nv, planes, share, cols), BF16),
             pltpu.VMEM((nv, cols, cols), BF16),
             pltpu.VMEM((1, bricks), jnp.int32),
-            dma((2, 2, CHUNKS)),
-            dma((2, 2, CHUNKS)),
+            dma((2, CHUNKS)),
+            dma((2, CHUNKS)),
+            dma((2, 2)),
+            dma((2, 2)),
+            dma((nv, 2, 2)),
+            dma((nv, 2, 2)),
             dma((n,)),
             dma((n,)),
             dma((n,)),
@@ -431,7 +477,7 @@
         ),
     )(
         estimate.reshape(planes * rows, cols),
-        raw_bricks.reshape(bricks, wide),
+        raw_bricks.reshape(bricks * cells, cols),
         brick_slab.reshape(1, bricks),
         brick_pos,
         off_z, frac_z, off_y, frac_y, off_x, frac_x, psf_z, psf_y, psf_x,

time: 108 us -> 103 us (0.954)
  Pallas kernels: 99.3 us -> 91.1 us
  local copies, waits for them, and re-layouts: 7.54 us -> 11 us
    pallas_call x1, Pallas kernels: 99.3 us -> 91.1 us  [shards(): pl.pallas_call(functools.partial(step, dims), out_shape=jax.ShapeDtypeStr...]
    unnamed x25 -> x27, local copies, waits for them, and re-layouts: 5.6 us -> 11 us
    reshape x1 -> x0, local copies, waits for them, and re-layouts: 1.94 us -> none  [shards(): raw_bricks.reshape(bricks, wide)]
where the time goes in v2:
time: 103 us; the launch traced here: 102 us
  Pallas kernels  91.1 us (88%)
  local copies, waits for them, and re-layouts  11 us (11%)
    pallas_call x1, Pallas kernels, shards(): pl.pallas_call(functools.partial(step, dims), out_shape=jax.ShapeDtypeStr...  91.1 us
    unnamed x27, local copies, waits for them, and re-layouts  11 us

profile of v2, /device:TPU:12, one launch (start us, length us, event | category | flops | bytes accessed | tf_op | source)
XLA Modules:
  0.0 102.2 jit_solution(5426780294890801244)
XLA Ops:
  0.0 0.0 copy-start
  0.0 1.6 %copy-done = f32[32,128,128]{2,1,0:T(8,128)S(1)} copy-done((f32[32,128,128]{2,1,0:T(8,128)S(1)}, f32[32,128,128]{2,1,0:T(8,128)}, u32[]{:S(2)}) %copy-start) | copy-done | bytes 2097176
  1.6 0.0 copy-start.1
  1.6 1.2 %copy-done.1 = bf16[1,512,4,2,128]{4,3,2,1,0:T(2,128)(2,1)S(1)} copy-done((bf16[1,512,4,2,128]{4,3,2,1,0:T(2,128)(2,1)S(1)}, bf16[1,512,4,2,128]{4,3,2,1,0:T(2,128)(2,1)}, u32[]{:S(2)}) %copy-start.1) | copy-done | bytes 1048600
  2.8 0.0 copy-start.2
  2.8 0.7 copy-done.2
  3.5 0.0 copy-start.3
  3.5 0.7 copy-done.3
  4.2 0.0 copy-start.4
  4.2 0.7 copy-done.4
  4.8 0.0 copy-start.5
  4.8 0.7 copy-done.5
  5.5 0.0 copy-start.6
  5.5 0.7 copy-done.6
  6.1 0.0 copy-start.7
  6.2 0.7 copy-done.7
  6.8 0.0 copy-start.8
  6.8 0.7 copy-done.8
  7.5 0.0 copy-start.9
  7.5 0.7 copy-done.9
  8.1 0.0 copy-start.10
  8.1 0.7 copy-done.10
  8.8 0.0 copy-start.11
  8.8 0.7 copy-done.11
  9.4 0.0 copy-start.12
  9.4 0.7 copy-done.12
  10.1 91.1 %shard_map.127 = f32[32,64,128]{2,1,0:T(8,128)S(1)} custom-call(f32[4096,128]{1,0:T(8,128)S(1)} %bitcast.3, bf16[4096,128]{1,0:T(8,128)(2,1)S(1)} %bitcast.4, s32[1,512]{1,0:T(1,128)S(1)} %bitcast.5, s32[1,512]{1,0:T(1,128)S(1)} %copy-done.3, s32[1,4]{1,0:T(1,128)S(1)} %copy-done.4, f32[1,4]{1,0:T(1,128)S(1)} %copy-done.5, s32[1,2]{1,0:T(1,128)S(1)} %copy-done.6, ...), custom_call_target="tpu_custom_call" | custom-call | tf_op jit(solution)/shard_map/pallas_call | solution.py:435
  101.2 1.0 copy.15
Async XLA Ops:
  0.0 1.6 %copy-start = (f32[32,128,128]{2,1,0:T(8,128)S(1)}, f32[32,128,128]{2,1,0:T(8,128)}, u32[]{:S(2)}) copy-start(f32[32,128,128]{2,1,0:T(8,128)} %param.13) | copy-start | bytes 6291460
  1.6 1.2 %copy-start.1 = (bf16[1,512,4,2,128]{4,3,2,1,0:T(2,128)(2,1)S(1)}, bf16[1,512,4,2,128]{4,3,2,1,0:T(2,128)(2,1)}, u32[]{:S(2)}) copy-start(bf16[1,512,4,2,128]{4,3,2,1,0:T(2,128)(2,1)} %param.14) | copy-start | bytes 3145732
  2.8 0.7 copy-start.2
  3.5 0.7 copy-start.3
  4.2 0.7 copy-start.4
  4.8 0.7 copy-start.5
  5.5 0.7 copy-start.6
  6.1 0.7 copy-start.7
  6.8 0.7 copy-start.8
  7.5 0.7 copy-start.9
  8.1 0.7 copy-start.10
  8.8 0.7 copy-start.11
  9.4 0.7 copy-start.12

commit v3 on v2

--- a/solution.py
+++ b/solution.py
@@ -34,6 +34,19 @@
 
 def step(
     dims,
+    *refs,
+):
+    operands, out, fetched, fetch_sem = refs[:13], refs[13], refs[14:27], refs[27]
+    est, raw, slab, pos, off_z, frac_z, off_y, frac_y, off_x, frac_x, psf_z, psf_y, psf_x = fetched
+    body(
+        dims, operands, fetched, fetch_sem,
+        est, raw, slab, pos, off_z, frac_z, off_y, frac_y, off_x, frac_x, psf_z, psf_y, psf_x,
+        out, *refs[28:],
+    )
+
+
+def body(
+    dims, operands, fetched, fetch_sem,
     est, raw, slab, pos, off_z, frac_z, off_y, frac_y, off_x, frac_x, psf_z, psf_y, psf_x,
     out,
     pad1, pad2, work, blurred, joined, weights, by_cell, mixed, outgoing, arrived, pos_out, pos_in, pos_row,
@@ -58,6 +71,12 @@
     me = lax.axis_index("gz")
     mv = lax.axis_index("view")
 
+    fetches = [
+        pltpu.make_async_copy(operands[i], fetched[i], fetch_sem.at[i]) for i in range(len(operands))
+    ]
+    for fetch in fetches:
+        fetch.start()
+
     barrier = pltpu.get_barrier_semaphore()
 
     @pl.loop(1, n)
@@ -74,6 +93,7 @@
             y = start + i
             pad[y, pl.ds(planes, planes), :] = source[pl.ds(y, planes, stride=rows), :].astype(BF16)
 
+    fetches[0].wait()
     own_rows(est, pad1, 0, rows)
 
     pl.semaphore_wait(barrier, n - 1 + nv - 1)
@@ -133,6 +153,8 @@
         for pad in (pad1, pad2):
             pad[:, pl.ds(2 * planes, planes), :] = jnp.zeros((rows, planes, cols), BF16)
 
+    for fetch in fetches[1:]:
+        fetch.wait()
     source = iota((cols, cols), 0)
     low = (1.0 - frac_x[...]).astype(BF16).astype(F32)
     high = frac_x[...].astype(BF16).astype(F32)
@@ -432,12 +454,20 @@
     dims = (planes, rows, cols, depth, height, bricks, n, nv, taps_z, taps_l)
     vmem = pl.BlockSpec(memory_space=pltpu.VMEM)
     dma = pltpu.SemaphoreType.DMA
+    operands = (
+        estimate.reshape(planes * rows, cols),
+        raw_bricks.reshape(bricks * cells, cols),
+        brick_slab.reshape(1, bricks),
+        brick_pos,
+        off_z, frac_z, off_y, frac_y, off_x, frac_x, psf_z, psf_y, psf_x,
+    )
     return pl.pallas_call(
         functools.partial(step, dims),
         out_shape=jax.ShapeDtypeStruct((planes, share, cols), F32),
-        in_specs=[vmem] * 13,
+        in_specs=[pl.BlockSpec(memory_space=pltpu.HBM)] * 13,
         out_specs=vmem,
-        scratch_shapes=[
+        scratch_shapes=[pltpu.VMEM(o.shape, o.dtype) for o in operands] + [
+            dma((13,)),
             pltpu.VMEM((rows, 3 * planes, cols), BF16),
             pltpu.VMEM((rows, 3 * planes, cols), BF16),
             pltpu.VMEM((max(rows * planes, bricks * cells), cols), F32),
@@ -473,15 +503,9 @@
             dma((2,)),
         ],
         compiler_params=pltpu.CompilerParams(
-            collective_id=0, has_side_effects=True, vmem_limit_bytes=48 * 1024 * 1024
+            collective_id=0, has_side_effects=True, vmem_limit_bytes=63 * 1024 * 1024
         ),
-    )(
-        estimate.reshape(planes * rows, cols),
-        raw_bricks.reshape(bricks * cells, cols),
-        brick_slab.reshape(1, bricks),
-        brick_pos,
-        off_z, frac_z, off_y, frac_y, off_x, frac_x, psf_z, psf_y, psf_x,
-    )
+    )(*operands)
 
 
 def solution(mesh):

time: 103 us -> 95 us (0.922)
  local copies, waits for them, and re-layouts: 11 us -> 2.31 us
  Pallas kernels: 91.1 us -> 92.6 us
    unnamed x27 -> x1, local copies, waits for them, and re-layouts: 11 us -> 2.31 us
    pallas_call x1, Pallas kernels: 91.1 us -> 92.6 us  [shards(): pl.pallas_call(functools.partial(step, dims), out_shape=jax.ShapeDtypeStr...]
where the time goes in v3:
time: 95 us; the launch traced here: 94.9 us
  Pallas kernels  92.6 us (97%)
  local copies, waits for them, and re-layouts  2.31 us (2%)
    pallas_call x1, Pallas kernels, shards(): pl.pallas_call(functools.partial(step, dims), out_shape=jax.ShapeDtypeStr...  92.6 us
    unnamed x1, local copies, waits for them, and re-layouts  2.31 us

profile of v3, /device:TPU:12, one launch (start us, length us, event | category | flops | bytes accessed | tf_op | source)
XLA Modules:
  0.0 94.9 jit_solution(8616220853198600932)
XLA Ops:
  0.0 92.6 %shard_map.127 = f32[32,64,128]{2,1,0:T(8,128)} custom-call(f32[4096,128]{1,0:T(8,128)} %bitcast.3, bf16[4096,128]{1,0:T(8,128)(2,1)} %bitcast.4, s32[1,512]{1,0:T(1,128)} %bitcast.5, s32[1,512]{1,0:T(1,128)} %refs_3_.1, s32[1,4]{1,0:T(1,128)} %refs_4_.1, f32[1,4]{1,0:T(1,128)} %refs_5_.1, s32[1,2]{1,0:T(1,128)} %refs_6_.1, f32[1,2]{1,0:T(1,128)} %refs_7_.1, ...), custom_call_target="tpu_custom_call" | custom-call | tf_op jit(solution)/shard_map/pallas_call | solution.py:464
  92.6 2.3 %copy.15 = f32[32,64,128]{2,1,0:T(8,128)} copy(f32[32,64,128]{2,1,0:T(8,128)} %shard_map.127) | data formatting | bytes 2097152

commit v4 on v3

--- a/solution.py
+++ b/solution.py
@@ -50,7 +50,7 @@
     est, raw, slab, pos, off_z, frac_z, off_y, frac_y, off_x, frac_x, psf_z, psf_y, psf_x,
     out,
     pad1, pad2, work, blurred, joined, weights, by_cell, mixed, outgoing, arrived, pos_out, pos_in, pos_row,
-    placer, back, from_views, x_tables, slot_scr,
+    placer, back_y, back, from_views, x_tables, slot_scr,
     halo_send, halo_recv, share_send, share_recv, pass_send, pass_recv, brick_send, brick_recv, pos_send, pos_recv, view_send, view_recv,
     xt_send, xt_recv, own_sem,
 ):
@@ -65,7 +65,6 @@
     half = taps_z // 2
     lat = taps_l // 2
     share = rows // nv
-    part = rows // CHUNKS
     zpart = planes // CHUNKS
     piece = share // 2
     me = lax.axis_index("gz")
@@ -136,8 +135,21 @@
             device_id_type=pl.DeviceIdType.MESH,
         )
 
+    if nv == 2 and lat <= 16 and share > 16:
+        lead = (share + 16) // height
+        rest = block_rows - lead
+        segments = [(d, (1 - mv) * rest, lead) for d in range(height)]
+        later = [(d, mv * lead, rest) for d in range(height)]
+    else:
+        segments = [(d, 0, block_rows) for d in range(height)]
+        later = []
+
+    def segment_start(d, at):
+        return pl.multiple_of(d * block_rows + at, 8)
+
     def halo(c):
-        return neighbours(c * part, part, pad2, halo_send, halo_recv, c)
+        d, at, count = (segments + later)[c]
+        return neighbours(segment_start(d, at), count, pad2, halo_send, halo_recv, c)
 
     for c in range(2):
         copy = share_copy(c)
@@ -242,7 +254,7 @@
 
     ii, jj = iota((rows, rows), 0), iota((rows, rows), 1)
     fy = tap_table(psf_y, taps_l, jj - true_row(ii) + lat)
-    by = tap_table(psf_y, taps_l, ii - true_row(jj) + lat)
+    back_y[...] = tap_table(psf_y, taps_l, ii - true_row(jj) + lat)
     ci, cj = iota((cols, cols), 0), iota((cols, cols), 1)
     fx = tap_table(psf_x, taps_l, ci - cj + lat)
     x_tables[mv] = tap_table(psf_x, taps_l, cj - ci + lat)
@@ -265,7 +277,7 @@
         xt_copy(lax.rem(mv + i, nv), mv).start()
 
     def z_pass(pad, table, start, count):
-        @pl.loop(0, count // 4, unroll=4)
+        @pl.loop(0, count // 4, unroll=2)
         def _(i):
             y = start + i * 4
             block = jnp.concatenate([pad[y + j] for j in range(4)], axis=1)
@@ -340,24 +352,35 @@
                 block_planes, block_rows, cols
             )
 
-    for c in range(CHUNKS):
-        d, at_row = c * part // block_rows, c * part % block_rows
+    for c, (d, at, count) in enumerate(segments + later):
+        start = segment_start(d, at)
 
         @pl.loop(0, block_planes)
         def _(i):
             for k in range(depth):
                 z = i * depth + k
-                work[pl.ds(z * rows + c * part, part), :] = (
-                    1.0 + joined[i, k, d, at_row:at_row + part, :]
-                ) / blurred[z, c * part:(c + 1) * part, :]
-
-        own_rows(work, pad2, c * part, part)
+                work[pl.ds(pl.multiple_of(z * rows + start, 8), count), :] = (
+                    1.0 + joined[i, k, d, pl.ds(pl.multiple_of(at, 8), count), :]
+                ) / blurred[z, pl.ds(start, count), :]
+
+        own_rows(work, pad2, start, count)
         copy = halo(c)
         on_sides(copy(0).start, copy(1).start)
-    for c in range(CHUNKS):
+
+    def arrive(c):
+        d, at, count = (segments + later)[c]
         copy = halo(c)
         on_sides(copy(0).wait_recv, copy(1).wait_recv, arriving=True)
-        z_pass(pad2, bz, c * part, part)
+        z_pass(pad2, bz, segment_start(d, at), count)
+
+    def back_rows(view, z):
+        at = pl.multiple_of(view * share, share)
+        along_y = y_pass(back_y[pl.ds(at, share), :], z)
+        for j in range(2):
+            back[z + j, pl.ds(at, share), :] = along_y[:, j * cols:(j + 1) * cols]
+
+    for c in range(len(segments)):
+        arrive(c)
 
     def view_copy(peer, owner, c):
         return pltpu.make_async_remote_copy(
@@ -370,16 +393,21 @@
         )
 
     for c in range(CHUNKS):
-        @pl.loop(0, zpart // 2, unroll=4)
-        def _(i):
-            z = c * zpart + 2 * i
-            along_y = y_pass(by, z)
-            for j in range(2):
-                back[z + j] = along_y[:, j * cols:(j + 1) * cols]
-
-        @pl.loop(1, nv)
-        def _(i):
-            view_copy(lax.rem(mv + i, nv), mv, c).start()
+        for v in range(1, nv):
+            peer = lax.rem(mv + v, nv)
+
+            @pl.loop(0, zpart // 2, unroll=4)
+            def _(i):
+                back_rows(peer, c * zpart + 2 * i)
+
+            view_copy(peer, mv, c).start()
+
+    for c in range(len(later)):
+        arrive(len(segments) + c)
+
+    @pl.loop(0, planes // 2, unroll=4)
+    def _(i):
+        back_rows(mv, 2 * i)
 
     first = pl.multiple_of(mv * share, share)
 
@@ -417,10 +445,10 @@
         copy = share_copy(c)
         on_sides(copy(0).wait_send, copy(1).wait_send)
         on_sides(lambda: pass_sent(0, c), lambda: pass_sent(1, c), arriving=True)
-    for c in range(CHUNKS):
+    for c in range(len(segments + later)):
         copy = halo(c)
         on_sides(copy(0).wait_send, copy(1).wait_send)
-
+    for c in range(CHUNKS):
         @pl.loop(1, nv)
         def _(i):
             view_copy(lax.rem(mv + i, nv), mv, c).wait_send()
@@ -482,12 +510,13 @@
             pltpu.VMEM((n, 16, 128), BF16),
             pltpu.VMEM((8, slots), F32),
             pltpu.VMEM((places, slots), BF16),
+            pltpu.VMEM((rows, rows), BF16),
             pltpu.VMEM((planes, rows, cols), BF16),
             pltpu.VMEM((nv, planes, share, cols), BF16),
             pltpu.VMEM((nv, cols, cols), BF16),
             pltpu.VMEM((1, bricks), jnp.int32),
-            dma((2, CHUNKS)),
-            dma((2, CHUNKS)),
+            dma((2, 2 * height)),
+            dma((2, 2 * height)),
             dma((2, 2)),
             dma((2, 2)),
             dma((nv, 2, 2)),

time: 95 us -> 91.2 us (0.960)
  Pallas kernels: 92.6 us -> 88.8 us
    pallas_call x1, Pallas kernels: 92.6 us -> 88.8 us  [shards(): pl.pallas_call(functools.partial(step, dims), out_shape=jax.ShapeDtypeStr...]
where the time goes in v4:
time: 91.2 us; the launch traced here: 91.1 us
  Pallas kernels  88.8 us (97%)
  local copies, waits for them, and re-layouts  2.31 us (3%)
    pallas_call x1, Pallas kernels, shards(): pl.pallas_call(functools.partial(step, dims), out_shape=jax.ShapeDtypeStr...  88.8 us
    unnamed x1, local copies, waits for them, and re-layouts  2.31 us

profile of v4, /device:TPU:12, one launch (start us, length us, event | category | flops | bytes accessed | tf_op | source)
XLA Modules:
  0.0 91.1 jit_solution(7468531147039338019)
XLA Ops:
  0.0 88.8 %shard_map.127 = f32[32,64,128]{2,1,0:T(8,128)} custom-call(f32[4096,128]{1,0:T(8,128)} %bitcast.3, bf16[4096,128]{1,0:T(8,128)(2,1)} %bitcast.4, s32[1,512]{1,0:T(1,128)} %bitcast.5, s32[1,512]{1,0:T(1,128)} %refs_3_.1, s32[1,4]{1,0:T(1,128)} %refs_4_.1, f32[1,4]{1,0:T(1,128)} %refs_5_.1, s32[1,2]{1,0:T(1,128)} %refs_6_.1, f32[1,2]{1,0:T(1,128)} %refs_7_.1, ...), custom_call_target="tpu_custom_call" | custom-call | tf_op jit(solution)/shard_map/pallas_call | solution.py:492
  88.8 2.3 %copy.15 = f32[32,64,128]{2,1,0:T(8,128)} copy(f32[32,64,128]{2,1,0:T(8,128)} %shard_map.127) | data formatting | bytes 2097152

commit v5 on v4

--- a/solution.py
+++ b/solution.py
@@ -49,7 +49,7 @@
     dims, operands, fetched, fetch_sem,
     est, raw, slab, pos, off_z, frac_z, off_y, frac_y, off_x, frac_x, psf_z, psf_y, psf_x,
     out,
-    pad1, pad2, work, blurred, joined, weights, by_cell, mixed, outgoing, arrived, pos_out, pos_in, pos_row,
+    pad1, pad2, work, inverse, joined, weights, by_cell, mixed, outgoing, arrived, pos_out, pos_in, pos_row,
     placer, back_y, back, from_views, x_tables, slot_scr,
     halo_send, halo_recv, share_send, share_recv, pass_send, pass_recv, brick_send, brick_recv, pos_send, pos_recv, view_send, view_recv,
     xt_send, xt_recv, own_sem,
@@ -239,9 +239,11 @@
 
     @pl.loop(1, n)
     def _(i):
-        peer = lax.rem(me + i, n)
-        brick_copy(peer, me).start()
-        pos_copy(peer, me).start()
+        pos_copy(lax.rem(me + i, n), me).start()
+
+    @pl.loop(1, n)
+    def _(i):
+        brick_copy(lax.rem(me + i, n), me).start()
 
     mine = pl.ds(pl.multiple_of(me * cap, cap), cap)
     own_bricks = pltpu.make_async_copy(outgoing.at[mine, :], arrived.at[mine, :], own_sem.at[0])
@@ -320,7 +322,7 @@
     def _(i):
         along_y = y_pass(fy, 2 * i)
         for j in range(2):
-            blurred[2 * i + j] = jnp.dot(
+            inverse[2 * i + j] = 1.0 / jnp.dot(
                 along_y[:, j * cols:(j + 1) * cols], fx, preferred_element_type=F32
             )
 
@@ -361,7 +363,7 @@
                 z = i * depth + k
                 work[pl.ds(pl.multiple_of(z * rows + start, 8), count), :] = (
                     1.0 + joined[i, k, d, pl.ds(pl.multiple_of(at, 8), count), :]
-                ) / blurred[z, pl.ds(start, count), :]
+                ) * inverse[z, pl.ds(start, count), :]
 
         own_rows(work, pad2, start, count)
         copy = halo(c)

time: 91.2 us -> 91.2 us (level)
  no operation moved by 1% of the time
where the time goes in v5:
time: 91.2 us; the launch traced here: 91.1 us
  Pallas kernels  88.8 us (97%)
  local copies, waits for them, and re-layouts  2.31 us (3%)
    pallas_call x1, Pallas kernels, shards(): pl.pallas_call(functools.partial(step, dims), out_shape=jax.ShapeDtypeStr...  88.8 us
    unnamed x1, local copies, waits for them, and re-layouts  2.31 us

profile of v5, /device:TPU:12, one launch (start us, length us, event | category | flops | bytes accessed | tf_op | source)
XLA Modules:
  0.0 91.1 jit_solution(10289059053939584942)
XLA Ops:
  0.0 88.8 %shard_map.127 = f32[32,64,128]{2,1,0:T(8,128)} custom-call(f32[4096,128]{1,0:T(8,128)} %bitcast.3, bf16[4096,128]{1,0:T(8,128)(2,1)} %bitcast.4, s32[1,512]{1,0:T(1,128)} %bitcast.5, s32[1,512]{1,0:T(1,128)} %refs_3_.1, s32[1,4]{1,0:T(1,128)} %refs_4_.1, f32[1,4]{1,0:T(1,128)} %refs_5_.1, s32[1,2]{1,0:T(1,128)} %refs_6_.1, f32[1,2]{1,0:T(1,128)} %refs_7_.1, ...), custom_call_target="tpu_custom_call" | custom-call | tf_op jit(solution)/shard_map/pallas_call | solution.py:494
  88.8 2.3 %copy.15 = f32[32,64,128]{2,1,0:T(8,128)} copy(f32[32,64,128]{2,1,0:T(8,128)} %shard_map.127) | data formatting | bytes 2097152

commit v6 on v5

--- a/solution.py
+++ b/solution.py
@@ -241,9 +241,12 @@
     def _(i):
         pos_copy(lax.rem(me + i, n), me).start()
 
-    @pl.loop(1, n)
-    def _(i):
-        brick_copy(lax.rem(me + i, n), me).start()
+    by_four = n // 4 if n % 4 == 0 else 0
+    orders = [(0, by_four, 4, 2), (0, 2 * by_four, 2, 1), (1, by_four, 4, 0)]
+    for begin, end, stride, offset in orders if by_four else [(1, n, 1, 0)]:
+        @pl.loop(begin, end)
+        def _(i):
+            brick_copy(lax.rem(me + i * stride + offset, n), me).start()
 
     mine = pl.ds(pl.multiple_of(me * cap, cap), cap)
     own_bricks = pltpu.make_async_copy(outgoing.at[mine, :], arrived.at[mine, :], own_sem.at[0])

time: 91.2 us -> 91.5 us (level)
  no operation moved by 1% of the time
where the time goes in v6:
time: 91.5 us; the launch traced here: 91.3 us
  Pallas kernels  89 us (97%)
  local copies, waits for them, and re-layouts  2.31 us (3%)
    pallas_call x1, Pallas kernels, shards(): pl.pallas_call(functools.partial(step, dims), out_shape=jax.ShapeDtypeStr...  89 us
    unnamed x1, local copies, waits for them, and re-layouts  2.31 us

profile of v6, /device:TPU:12, one launch (start us, length us, event | category | flops | bytes accessed | tf_op | source)
XLA Modules:
  0.0 91.3 jit_solution(16076564453905256360)
XLA Ops:
  0.0 89.0 %shard_map.127 = f32[32,64,128]{2,1,0:T(8,128)} custom-call(f32[4096,128]{1,0:T(8,128)} %bitcast.3, bf16[4096,128]{1,0:T(8,128)(2,1)} %bitcast.4, s32[1,512]{1,0:T(1,128)} %bitcast.5, s32[1,512]{1,0:T(1,128)} %refs_3_.1, s32[1,4]{1,0:T(1,128)} %refs_4_.1, f32[1,4]{1,0:T(1,128)} %refs_5_.1, s32[1,2]{1,0:T(1,128)} %refs_6_.1, f32[1,2]{1,0:T(1,128)} %refs_7_.1, ...), custom_call_target="tpu_custom_call" | custom-call | tf_op jit(solution)/shard_map/pallas_call | solution.py:497
  89.0 2.3 %copy.15 = f32[32,64,128]{2,1,0:T(8,128)} copy(f32[32,64,128]{2,1,0:T(8,128)} %shard_map.127) | data formatting | bytes 2097152
